TPU v7x, 512 devices: a whole 4x4x16 slice. The times are simulated.
512 devices in a mesh: col: 16 (over x, y), row: 32 (over z, core).
Axes of the slice: x: 4, y: 4, z: 16, core: 2. Of those that a mesh axis runs over, the one named last changes fastest.
Arguments:
- features: bfloat16 [65536, 256], P(('col', 'row')), may hold values from -6 to 6
- weight: bfloat16 [256, 256], replicated, may hold values from -0.375 to 0.375
- grad_out: bfloat16 [65536, 256], P(('col', 'row')), may hold values from -6 to 6
- tile_values: bfloat16 [16, 32, 96, 128, 128], P('col', 'row'), may hold values from -0.078125 to 0.078125
- tile_coords: int32 [16, 32, 2, 96], P('col', 'row'), may hold values from 0 to 31, as said below
- tile_count: int32 [16, 32], P('col', 'row'), may hold values from 1 to 96, as said below
Outputs:
- feature_grad: bfloat16 [65536, 256], P(('col', 'row'))
- weight_grad: float32 [256, 256], replicated
Inputs may be any that keep to these rules, and one draw needn't show every extreme that they name: tile_coords[c, r, 0, k] is below 16 and tile_coords[c, r, 1, k] below 32; the 96 pairs of one block are all different. `tile_count`: at least one block has exactly 96 live slots.
All inputs are finite; a program needn't handle non-finite values.
Results may differ from a plain program's by a relative error of at most 0.03.
Values may be sent and summed in bfloat16 or wider, within the bound.
A program may use at most 64 MiB of HBM per device.

v0:
```python
import math

import jax
import jax.numpy as jnp
from jax import lax
from jax.sharding import PartitionSpec as P


def forward_tiles(masked, tile_pairs, column_rows, row_tiles, tile_size):
    feat_width = column_rows.shape[1]
    picked = column_rows.reshape(-1, tile_size, feat_width)[tile_pairs[1]]
    product = jnp.einsum("sab,sbf->saf", masked, picked, preferred_element_type=jnp.float32)
    summed = jax.ops.segment_sum(product, tile_pairs[0], num_segments=row_tiles)
    return summed.reshape(row_tiles * tile_size, feat_width)


def backward_tiles(masked, tile_pairs, block_rows, col_tiles, tile_size):
    feat_width = block_rows.shape[1]
    picked = block_rows.reshape(-1, tile_size, feat_width)[tile_pairs[0]]
    product = jnp.einsum("sab,saf->sbf", masked, picked, preferred_element_type=jnp.float32)
    summed = jax.ops.segment_sum(product, tile_pairs[1], num_segments=col_tiles)
    return summed.reshape(col_tiles * tile_size, feat_width)


def activation_grad(agg_rows, grad_rows, weight):
    pre_act = jnp.dot(agg_rows, weight, preferred_element_type=jnp.float32)
    sigmoid_z = jax.nn.sigmoid(pre_act)
    factor = sigmoid_z * (1.0 + pre_act * (1.0 - sigmoid_z))
    return (grad_rows.astype(jnp.float32) * factor).astype(jnp.bfloat16)


def project_back(dz_rows, weight):
    return lax.dot_general(
        dz_rows, weight, (((1,), (1,)), ((), ())), preferred_element_type=jnp.float32
    ).astype(jnp.bfloat16)


def body(features, weight, grad_out, tile_values, tile_coords, tile_count):
    node_rows = features.shape[0]
    tile_size = tile_values.shape[-1]
    slot_count = tile_values.shape[2]
    col_devices = lax.axis_size("col")
    row_devices = lax.axis_size("row")
    row_tiles = node_rows * col_devices // tile_size
    col_tiles = node_rows * row_devices // tile_size
    tile_pairs = tile_coords[0, 0]
    live_slots = (jnp.arange(slot_count) < tile_count[0, 0]).astype(jnp.bfloat16)
    masked = tile_values[0, 0] * live_slots[:, None, None]
    column_rows = lax.all_gather(features, "row", axis=0, tiled=True)
    partial_rows = forward_tiles(masked, tile_pairs, column_rows, row_tiles, tile_size)
    agg_own = lax.psum_scatter(
        partial_rows.astype(jnp.bfloat16), "col", scatter_dimension=0, tiled=True
    )
    dz_own = activation_grad(agg_own, grad_out, weight)
    back_own = project_back(dz_own, weight)
    back_rows = lax.all_gather(back_own, "col", axis=0, tiled=True)
    local_weight = lax.dot_general(
        agg_own, dz_own, (((0,), (0,)), ((), ())), preferred_element_type=jnp.float32
    )
    scaling = 1.0 / math.sqrt(node_rows * col_devices * row_devices)
    weight_grad = lax.psum(local_weight, ("col", "row")) * scaling
    transposed = backward_tiles(masked, tile_pairs, back_rows, col_tiles, tile_size)
    feature_grad = lax.psum_scatter(
        transposed.astype(jnp.bfloat16), "row", scatter_dimension=0, tiled=True
    )
    return (feature_grad, weight_grad)


def solution(mesh):
    return jax.shard_map(
        body,
        mesh=mesh,
        in_specs=(
            P(("col", "row"), None),
            P(),
            P(("col", "row"), None),
            P("col", "row", None, None, None),
            P("col", "row", None, None),
            P("col", "row"),
        ),
        out_specs=(P(("col", "row"), None), P()),
        check_vma=False,
    )
```

profile of v0, /device:TPU:1, one launch (start us, length us, event | category | flops | bytes accessed | tf_op | source)
XLA Modules:
  0.0 846.0 jit_solution(12454247709626394916)
XLA Ops:
  7.2 0.0 copy-start
  7.2 0.0 all-gather.3.cloned.1.call-start
  7.2 0.7 all-gather.3.cloned.1.call-update
  7.9 0.0 reduce-scatter.3.cloned.1.call-start
  8.6 0.8 fusion.5
  9.4 0.8 slice_bitcast_fusion
  10.1 77.5 %all-gather.3.cloned.1.call-done = bf16[4096,256]{1,0:T(8,128)(2,1)} async-done(((bf16[128,256]{1,0:T(8,128)(2,1)}), bf16[4096,256]{1,0:T(8,128)(2,1)}) %all-gather.3.cloned.1.call-update) | async-done | bytes 2097168 | tf_op jit(solution)/shard_map/all_gather | solution.py:49
  87.7 7.7 gather_fusion
  95.4 9.2 %fusion.1 = f32[96,128,256]{2,1,0:T(8,128)} fusion(bf16[96,128,256]{2,1,0:T(8,128)(2,1)} %gather_fusion, bf16[1,1,96,128,128]{4,3,2,1,0:T(8,128)(2,1)S(1)} %copy-done.1, bf16[96]{0:T(256)(128)(2,1)S(1)} %compare_convert_fusion), kind=kOutput, calls=%fused_computation.6 | convolution fusion | flops 806879232 | bytes 22020288 | tf_op jit(solution)/shard_map/sab,sbf->saf/dot_general | solution.py:12
  104.6 0.2 broadcast_in_dim.10
  104.8 18.4 %scatter_fusion = f32[16,128,256]{2,1,0:T(8,128)S(1)} fusion(f32[16,128,256]{2,1,0:T(8,128)S(1)} %broadcast_in_dim.10, s32[96]{0:T(128)S(1)} %get-tuple-element.4, f32[96,128,256]{2,1,0:T(8,128)} %fusion.1), kind=kCustom, calls=%fused_computation.2 | custom fusion | flops 3145728 | bytes 37749120 | tf_op jit(solution)/shard_map/scatter-add | solution.py:13
  123.1 1.1 convert_element_type.30
  124.2 0.0 reduce-scatter.3.cloned.1.call-update
  124.3 0.0 all-gather.5.cloned.1.call-start
  124.3 83.2 %reduce-scatter.3.cloned.1.call-done = bf16[128,256]{1,0:T(8,128)(2,1)} async-done(((bf16[2048,256]{1,0:T(8,128)(2,1)}), bf16[128,256]{1,0:T(8,128)(2,1)}) %reduce-scatter.3.cloned.1.call-update) | async-done | bytes 65552 | tf_op jit(solution)/shard_map/reduce_scatter | solution.py:51
  207.6 1.1 multiply_convert_fusion
  208.6 0.8 convolution_convert_fusion
  209.4 0.0 all-gather.5.cloned.1.call-update
  209.5 0.0 all-reduce.2.cloned.1.call-start
  209.5 1.8 fusion.6
  211.3 0.0 all-reduce.2.cloned.1.call-update
  211.3 0.0 reduce-scatter.5.cloned.1.call-start
  211.4 57.9 %all-gather.5.cloned.1.call-done = bf16[2048,256]{1,0:T(8,128)(2,1)} async-done(((bf16[128,256]{1,0:T(8,128)(2,1)}), bf16[2048,256]{1,0:T(8,128)(2,1)}) %all-gather.5.cloned.1.call-update) | async-done | bytes 1048592 | tf_op jit(solution)/shard_map/all_gather | solution.py:56
  269.3 7.3 gather_fusion.1
  276.6 10.1 %fusion = f32[96,128,256]{2,1,0:T(8,128)} fusion(bf16[96,128,256]{2,1,0:T(8,128)(2,1)} %gather_fusion.1, bf16[1,1,96,128,128]{4,3,2,1,0:T(8,128)(2,1)S(1)} %copy-done.2, bf16[96]{0:T(256)(128)(2,1)S(1)} %compare_convert_fusion), kind=kOutput, calls=%fused_computation.5 | convolution fusion | flops 806879232 | bytes 22020288 | tf_op jit(solution)/shard_map/sab,saf->sbf/dot_general | solution.py:20
  286.7 2.4 broadcast_in_dim.4
  289.2 28.7 %scatter_fusion.1 = f32[32,128,256]{2,1,0:T(8,128)} fusion(f32[32,128,256]{2,1,0:T(8,128)} %broadcast_in_dim.4, s32[96]{0:T(128)S(1)} %get-tuple-element.5, f32[96,128,256]{2,1,0:T(8,128)} %fusion), kind=kCustom, calls=%fused_computation.3 | custom fusion | flops 3145728 | bytes 37749120 | tf_op jit(solution)/shard_map/scatter-add | solution.py:21
  317.9 3.8 convert_element_type.34
  321.7 0.0 reduce-scatter.5.cloned.1.call-update
  321.8 410.7 %all-reduce.2.cloned.1.call-done = f32[256,256]{1,0:T(8,128)} async-done(((f32[256,256]{1,0:T(8,128)}), f32[256,256]{1,0:T(8,128)}) %all-reduce.2.cloned.1.call-update) | async-done | bytes 262160 | tf_op jit(solution)/shard_map/psum | solution.py:61
  732.5 1.7 broadcast_multiply_fusion
  734.2 105.3 %reduce-scatter.5.cloned.1.call-done = bf16[128,256]{1,0:T(8,128)(2,1)} async-done(((bf16[4096,256]{1,0:T(8,128)(2,1)}), bf16[128,256]{1,0:T(8,128)(2,1)}) %reduce-scatter.5.cloned.1.call-update) | async-done | bytes 65552 | tf_op jit(solution)/shard_map/reduce_scatter | solution.py:63
  (10 shorter events, 0.0 us)
Async XLA Ops:
  7.2 200.4 %copy-start = (bf16[256,256]{1,0:T(8,128)(2,1)S(1)}, bf16[256,256]{1,0:T(8,128)(2,1)}, u32[]{:S(2)}) copy-start(bf16[256,256]{1,0:T(8,128)(2,1)} %param.7) | copy-start | bytes 393220
  7.2 80.5 %all-gather.3.cloned.1.call-start = ((), (), s32[]{:S(2)}) async-start(), calls=%async_computation.2 | async-start | bytes 2162688 | tf_op jit(solution)/shard_map/all_gather | solution.py:49
  7.9 199.6 %reduce-scatter.3.cloned.1.call-start = ((), (), s32[]{:S(2)}) async-start(), calls=%async_computation.3 | async-start | bytes 1114112 | tf_op jit(solution)/shard_map/reduce_scatter | solution.py:51
  87.7 7.7 copy-start.1
  104.8 102.8 %copy-start.3 = (bf16[128,256]{1,0:T(8,128)(2,1)S(1)}, bf16[128,256]{1,0:T(8,128)(2,1)}, u32[]{:S(2)}) copy-start(bf16[128,256]{1,0:T(8,128)(2,1)} %param.8) | copy-start | bytes 196612
  124.3 145.0 %all-gather.5.cloned.1.call-start = ((), (), s32[]{:S(2)}) async-start(), calls=%async_computation.4 | async-start | bytes 1114112 | tf_op jit(solution)/shard_map/all_gather | solution.py:56
  209.5 523.0 %all-reduce.2.cloned.1.call-start = ((), (), s32[]{:S(2)}) async-start(), calls=%async_computation.6 | async-start | bytes 524288 | tf_op jit(solution)/shard_map/psum | solution.py:61
  211.3 628.2 %reduce-scatter.5.cloned.1.call-start = ((), (), s32[]{:S(2)}) async-start(), calls=%async_computation.5 | async-start | bytes 2162688 | tf_op jit(solution)/shard_map/reduce_scatter | solution.py:63
  269.3 7.3 copy-start.2
Sparse Core Ops, SparseCore 0:
  10.1 77.5 all-gather.2
  124.4 83.1 reduce-scatter.2
  211.6 57.6 all-gather.4
  276.1 456.3 all-reduce.1
  735.7 103.7 reduce-scatter.4
where the time goes:
time: 849 us; the launch traced here: 846 us
  waiting for transfers between devices  736 us (87%)
  other arithmetic  54.5 us (6%)
  matrix products  22.9 us (3%)
  local copies, waits for them, and re-layouts  18.4 us (2%)
  between operations  14.5 us (2%)
    psum x1, waiting for transfers between devices, body(): weight_grad = lax.psum(local_weight, ('col', 'row')) * scaling  411 us
    reduce_scatter x1, waiting for transfers between devices, body(): lax.psum_scatter(transposed.astype(jnp.bfloat16), 'row', scatter_dimensio...  105 us
    reduce_scatter x1, waiting for transfers between devices, body(): lax.psum_scatter(partial_rows.astype(jnp.bfloat16), 'col', scatter_dimens...  83.2 us
    all_gather x1, waiting for transfers between devices, body(): column_rows = lax.all_gather(features, 'row', axis=0, tiled=True)  77.5 us
    all_gather x1, waiting for transfers between devices, body(): back_rows = lax.all_gather(back_own, 'col', axis=0, tiled=True)  57.9 us
    scatter-add x1, other arithmetic, backward_tiles(): summed = jax.ops.segment_sum(product, tile_pairs[1], num_segments=col_tiles)  28.7 us
    scatter-add x1, other arithmetic, forward_tiles(): summed = jax.ops.segment_sum(product, tile_pairs[0], num_segments=row_tiles)  18.4 us
  transfers between devices with their start and end apart: 5, of which 5 were waited for; matrix products, arithmetic and copies ran while one was open for 7% of the time, Pallas kernels for 0%

commit v1 on v0

v1 whole, which is shorter than its diff:
```python
import functools
import math

import jax
import jax.numpy as jnp
from jax import lax
from jax.experimental import pallas as pl
from jax.experimental.pallas import tpu as pltpu
from jax.sharding import PartitionSpec as P

MESH = pl.DeviceIdType.MESH
DMA = pltpu.SemaphoreType.DMA
BF = jnp.bfloat16
F32 = jnp.float32

SX, SY, SZ = 4, 4, 16
OFFS = (0, 1, -1, 2, -2, 3, -3, 4, -4, 5, -5, 6, -6, 7, -7, 8)
GROUPS = ((0, 1), (1, 5), (5, 9), (9, 13), (13, 16))
SLOT = {o: t for t, o in enumerate(OFFS)}
SLOT[-8] = SLOT[8]
NCOL = SX * SY


class Links:
    def __init__(self, send_sems, recv_sems):
        self.send_sems, self.recv_sems = send_sems, recv_sems
        self.used = 0
        self.sent = []

    def copy(self, src, dst, device):
        at = self.used
        self.used += 1
        return pltpu.make_async_remote_copy(
            src_ref=src,
            dst_ref=dst,
            send_sem=self.send_sems.at[at],
            recv_sem=self.recv_sems.at[at],
            device_id=device,
            device_id_type=MESH,
        )

    def start(self, src, dst, device):
        copy = self.copy(src, dst, device)
        copy.start()
        self.sent.append(copy)
        return copy

    def drain(self):
        for copy in self.sent:
            copy.wait_send()


def kernel(
    pieces,
    scaling,
    coords_ref,
    count_ref,
    feat_ref,
    weight_ref,
    grad_ref,
    tiles_ref,
    out_ref,
    wout_ref,
    inv_v,
    inv_s,
    tiles,
    tiles_t,
    feats,
    acc,
    part,
    part_rx,
    backs,
    own_t,
    pair_tx,
    pair_rx,
    leaf_tx,
    leaf_rx,
    chain_tx,
    chain_rx,
    w_loc,
    w_pair,
    w_sum,
    w_rx,
    w_z,
    w_piece,
    w_fin,
    local_sems,
    send_sems,
    recv_sems,
):
    col, row = lax.axis_index("col"), lax.axis_index("row")
    x, y = col // SY, col % SY
    z, core = row // 2, row % 2
    links = Links(send_sems, recv_sems)
    slots = tiles_ref.shape[0]
    tile = tiles_ref.shape[1]
    half = tile // 2

    def at_z(offset):
        return (col, lax.rem(z + offset + SZ, SZ) * 2 + core)

    def col_at(dx, dy):
        return lax.rem(x + dx + SX, SX) * SY + lax.rem(y + dy + SY, SY)

    partner = (col, z * 2 + 1 - core)
    shifts = [(d // SY, d % SY) for d in range(1, NCOL)]

    barrier = pltpu.get_barrier_semaphore()
    greeted = [at_z(o) for o in (1, -1, 2, -2)] + [partner]
    greeted += [(col_at(dx, dy), row) for dx, dy in shifts]
    for device in greeted:
        pl.semaphore_signal(barrier, inc=1, device_id=device, device_id_type=MESH)

    load_tiles = pltpu.make_async_copy(
        tiles_ref, tiles.at[pl.ds(1, slots)], local_sems.at[0]
    )
    load_tiles.start()
    feats[0, 0] = feat_ref[...]
    pl.semaphore_wait(barrier, len(greeted))

    ahead = {}
    rows_of = tile // pieces

    def rows(p):
        return pl.ds(p * rows_of, rows_of)

    def forward(buf, key, dist, side, p, whole):
        src = SLOT[side * dist]
        for hop in (2, 1):
            far = dist + hop
            if far > 8:
                continue
            if far == 8 and (p < whole // 2) != (side == 1):
                continue
            dst = SLOT[side * far]
            ahead[key, side * far, p] = links.start(
                buf(src, p), buf(dst, p), at_z(side * hop)
            )

    def feat_at(t, p):
        return feats.at[t, 0, rows(p)]

    crossed = {}

    def cross(t, p):
        crossed[t, p] = links.start(
            feats.at[t, 0, rows(p)], feats.at[t, 1, rows(p)], partner
        )

    for p in range(pieces):
        for side in (1, -1):
            forward(feat_at, "f", 0, side, p, pieces)
    for p in range(pieces):
        cross(0, p)

    tile_row = lax.broadcasted_iota(jnp.int32, inv_v.shape, 0)
    tile_col = lax.broadcasted_iota(jnp.int32, inv_v.shape, 1)
    live = count_ref[0, 0]

    def enter(k, table):
        hit = (tile_row == coords_ref[0, k]) & (tile_col == coords_ref[1, k])
        hit = hit & (jnp.full(inv_v.shape, k, jnp.int32) < live)
        return jnp.where(hit, k + 1, table)

    inv_v[...] = lax.fori_loop(
        0, slots, enter, jnp.zeros(inv_v.shape, jnp.int32), unroll=8
    )
    table_copy = pltpu.make_async_copy(inv_v, inv_s, local_sems.at[1])
    table_copy.start()
    tiles[0] = jnp.zeros(tiles.shape[1:], BF)
    tiles_t[0] = jnp.zeros(tiles.shape[1:], BF)
    table_copy.wait()
    load_tiles.wait()

    def column_tile(t, other):
        source = lax.rem(z - OFFS[t] + SZ, SZ)
        return source * 2 + (1 - core if other else core)

    block = 4

    def row_tile_of(q):
        d = NCOL - 1 - q
        return lax.rem(x + d // SY, SX) * SY + lax.rem(y + d % SY, SY)

    def product(lo, hi, q0):
        columns = [column_tile(t, o) for t in range(lo, hi) for o in (0, 1)]
        lhs = []
        for a in range(block):
            i = row_tile_of(q0 + a)
            lhs.append(jnp.concatenate([tiles[inv_s[i, j]] for j in columns], axis=1))
        rhs = feats[lo:hi].reshape((hi - lo) * 2 * tile, -1)
        return jnp.dot(
            jnp.concatenate(lhs, axis=0), rhs, preferred_element_type=F32
        )

    def accumulate(lo, hi):
        def one(b, carry):
            at = pl.ds(pl.multiple_of(b * block * tile, block * tile), block * tile)
            if lo == 0:
                acc[at] = product(lo, hi, b * block)
            else:
                acc[at] += product(lo, hi, b * block)
            return carry

        lax.fori_loop(0, NCOL // block, one, 0)

    def flip(k, carry):
        tiles_t[k + 1] = tiles[k + 1].T
        return carry

    for s, (lo, hi) in enumerate(GROUPS):
        if s:
            for p in range(pieces):
                for side in (1, -1):
                    key = ("f", side * 2 * s, p)
                    if key in ahead:
                        ahead[key].wait_recv()
                        if s < 4:
                            forward(feat_at, "f", 2 * s, side, p, pieces)
                        cross(SLOT[side * 2 * s], p)
                for side in (1, -1):
                    ahead["f", side * (2 * s - 1), p].wait_recv()
                    cross(SLOT[side * (2 * s - 1)], p)
            before_lo, before_hi = GROUPS[s - 1]
        else:
            lax.fori_loop(0, slots, flip, 0, unroll=4)
            continue
        for t in range(before_lo, before_hi):
            for p in range(pieces):
                crossed[t, p].wait_recv()
        accumulate(before_lo, before_hi)

    lo, hi = GROUPS[-1]
    for t in range(lo, hi):
        for p in range(pieces):
            crossed[t, p].wait_recv()

    arrivals = {}
    for b in range(NCOL // block):
        at = pl.ds(b * block * tile, block * tile)
        total = acc[at] + product(lo, hi, b * block)
        acc[at] = total
        for a in range(block):
            q = b * block + a
            d = NCOL - 1 - q
            if d:
                part[d - 1] = total[a * tile : (a + 1) * tile].astype(BF)
                arrivals[d] = links.start(
                    part.at[d - 1],
                    part_rx.at[d - 1],
                    (col_at(d // SY, d % SY), row),
                )
    agg = acc[pl.ds((NCOL - 1) * tile, tile)]
    for d in range(NCOL - 1, 0, -1):
        arrivals[d].wait_recv()
        agg = agg + part_rx[d - 1].astype(F32)
    agg = agg.astype(BF)

    weight = weight_ref[...]
    pre_act = jnp.dot(agg, weight, preferred_element_type=F32)
    sigmoid_z = jax.nn.sigmoid(pre_act)
    factor = sigmoid_z * (1.0 + pre_act * (1.0 - sigmoid_z))
    dz = (grad_ref[...].astype(F32) * factor).astype(BF)
    backs[0] = lax.dot_general(
        dz, weight, (((1,), (1,)), ((), ())), preferred_element_type=F32
    ).astype(BF)
    for d in range(NCOL - 1, 0, -1):
        arrivals[d] = links.start(
            backs.at[0], backs.at[d], (col_at(d // SY, d % SY), row)
        )
    local_weight = lax.dot_general(
        agg, dz, (((0,), (0,)), ((), ())), preferred_element_type=F32
    )
    for h in range(2):
        w_loc[h] = local_weight[:, h * 128 : (h + 1) * 128].reshape(NCOL, -1, 128)

    w_cross = links.start(w_loc.at[1 - core], w_pair, partner)
    w_cross.wait_recv()
    w_sum[...] = w_loc[core] + w_pair[...]
    w_arrivals = {}
    for d in range(NCOL - 1, 0, -1):
        to = col_at(d // SY, d % SY)
        w_arrivals[d] = links.start(w_sum.at[to], w_rx.at[d - 1], (to, row))

    for d in range(NCOL - 1, 0, -1):
        arrivals[d].wait_recv()

    def back_tile_of(d):
        return lax.rem(x - d // SY + SX, SX) * SY + lax.rem(y - d % SY + SY, SY)

    def transposed(columns):
        lhs = []
        for j in columns:
            lhs.append(
                jnp.concatenate(
                    [tiles_t[inv_s[back_tile_of(d), j]] for d in range(NCOL)], axis=1
                )
            )
        return jnp.dot(
            jnp.concatenate(lhs, axis=0),
            backs[...].reshape(NCOL * tile, -1),
            preferred_element_type=F32,
        )

    pair = {}

    def compute(offsets):
        for t0 in range(0, len(offsets), 2):
            some = offsets[t0 : t0 + 2]
            targets = [lax.rem(z + o + SZ, SZ) * 2 for o in some]
            terms = transposed(
                [t + 1 - core for t in targets] + [t + core for t in targets]
            )
            for n, o in enumerate(some):
                t = SLOT[o]
                pair_tx[t] = terms[n * tile : (n + 1) * tile].astype(BF)
                pair[t] = links.start(pair_tx.at[t], pair_rx.at[t], partner)
                m = n + len(some)
                own_t[t] = terms[m * tile : (m + 1) * tile]

    def pair_sum(o):
        t = SLOT[o]
        pair[t].wait_recv()
        return own_t[t] + pair_rx[t].astype(F32)

    leaf, chain = {}, {}

    def send_leaves(dist):
        for n, side in enumerate((1, -1)):
            m = dist // 2
            leaf_tx[n, m] = pair_sum(side * dist).astype(BF)
            leaf[side, dist] = links.start(
                leaf_tx.at[n, m], leaf_rx.at[n, m], at_z(side)
            )

    def send_chain(dist):
        m = dist // 2 - 1
        if dist == 8:
            total = pair_sum(8).astype(BF)
            for n, side in enumerate((1, -1)):
                chain_tx[n, m, n * half : (n + 1) * half] = total[
                    n * half : (n + 1) * half
                ]
                chain[side, dist] = links.start(
                    chain_tx.at[n, m, pl.ds(n * half, half)],
                    chain_rx.at[n, m, pl.ds(n * half, half)],
                    at_z(2 * side),
                )
            return
        for n, side in enumerate((1, -1)):
            total = pair_sum(side * dist)
            leaf[side, dist + 1].wait_recv()
            total = total + leaf_rx[n, m + 1].astype(F32)
            chain[side, dist + 2].wait_recv()
            if dist == 6:
                mine = total[n * half : (n + 1) * half]
                mine = mine + chain_rx[n, m + 1, n * half : (n + 1) * half].astype(F32)
                rest = total[(1 - n) * half : (2 - n) * half]
                chain_tx[n, m, n * half : (n + 1) * half] = mine.astype(BF)
                chain_tx[n, m, (1 - n) * half : (2 - n) * half] = rest.astype(BF)
            else:
                total = total + chain_rx[n, m + 1].astype(F32)
                chain_tx[n, m] = total.astype(BF)
            chain[side, dist] = links.start(
                chain_tx.at[n, m], chain_rx.at[n, m], at_z(2 * side)
            )

    def w_at(t, p):
        return w_z.at[t]

    def w_round(s):
        for side in (1, -1):
            key = ("w", side * 2 * s, 0)
            if key in ahead:
                ahead[key].wait_recv()
                if s < 4:
                    forward(w_at, "w", 2 * s, side, 0, 1)
            ahead["w", side * (2 * s - 1), 0].wait_recv()

    compute([8, 7, -7])
    compute([6, -6, 5, -5])
    send_leaves(7)
    send_chain(8)
    w_total = w_sum[col]
    for d in range(NCOL - 1, 0, -1):
        w_arrivals[d].wait_recv()
        w_total = w_total + w_rx[d - 1]
    w_z[0] = w_total.astype(BF)
    for side in (1, -1):
        forward(w_at, "w", 0, side, 0, 1)
    send_leaves(5)
    compute([4, -4, 3, -3])
    compute([2, -2, 1, -1])
    send_leaves(3)
    send_chain(6)
    w_round(1)
    compute([0])
    send_leaves(1)
    w_round(2)
    send_chain(4)
    w_round(3)
    send_chain(2)
    w_round(4)
    w_total = w_z[0].astype(F32)
    for t in range(1, len(OFFS)):
        w_total = w_total + w_z[t].astype(F32)
    w_fin[core, col] = w_total * scaling
    for d in range(NCOL - 1, 0, -1):
        to = col_at(d // SY, d % SY)
        w_arrivals[d] = links.start(w_fin.at[core, col], w_fin.at[core, col], (to, row))
    total = pair_sum(0)
    for n, side in enumerate((1, -1)):
        leaf[side, 1].wait_recv()
        total = total + leaf_rx[n, 0].astype(F32)
    for n, side in enumerate((1, -1)):
        chain[side, 2].wait_recv()
        total = total + chain_rx[n, 0].astype(F32)
    out_ref[...] = total.astype(BF)
    for d in range(NCOL - 1, 0, -1):
        w_arrivals[d].wait_recv()
    w_cross = links.start(w_fin.at[core], w_fin.at[core], partner)
    w_cross.wait_recv()
    for h in range(2):
        wout_ref[:, h * 128 : (h + 1) * 128] = w_fin[h].reshape(-1, 128)
    links.drain()


PIECES = 2
COPIES = 256


def body(features, weight, grad_out, tile_values, tile_coords, tile_count):
    tile, width = features.shape
    slots = tile_values.shape[2]
    nodes = tile * lax.axis_size("col") * lax.axis_size("row")
    vmem = pl.BlockSpec(memory_space=pltpu.VMEM)
    smem = pl.BlockSpec(memory_space=pltpu.SMEM)
    square = (tile, tile)
    slab = (tile, width)
    w_rows = width // NCOL
    return pl.pallas_call(
        functools.partial(kernel, PIECES, 1.0 / math.sqrt(nodes)),
        out_shape=(
            jax.ShapeDtypeStruct(slab, BF),
            jax.ShapeDtypeStruct((width, width), F32),
        ),
        in_specs=[smem, smem, vmem, vmem, vmem, pl.BlockSpec(memory_space=pl.ANY)],
        out_specs=(vmem, vmem),
        scratch_shapes=[
            pltpu.VMEM((16, 128), jnp.int32),
            pltpu.SMEM((16, 128), jnp.int32),
            pltpu.VMEM((slots + 1,) + square, BF),
            pltpu.VMEM((slots + 1,) + square, BF),
            pltpu.VMEM((16, 2) + slab, BF),
            pltpu.VMEM((NCOL * tile, width), F32),
            pltpu.VMEM((NCOL - 1,) + slab, BF),
            pltpu.VMEM((NCOL - 1,) + slab, BF),
            pltpu.VMEM((NCOL,) + slab, BF),
            pltpu.VMEM((16,) + slab, F32),
            pltpu.VMEM((16,) + slab, BF),
            pltpu.VMEM((16,) + slab, BF),
            pltpu.VMEM((2, 4) + slab, BF),
            pltpu.VMEM((2, 4) + slab, BF),
            pltpu.VMEM((2, 4) + slab, BF),
            pltpu.VMEM((2, 4) + slab, BF),
            pltpu.VMEM((2, NCOL, w_rows, 128), F32),
            pltpu.VMEM((NCOL, w_rows, 128), F32),
            pltpu.VMEM((NCOL, w_rows, 128), F32),
            pltpu.VMEM((NCOL - 1, w_rows, 128), F32),
            pltpu.VMEM((16, w_rows, 128), BF),
            pltpu.VMEM((w_rows, 128), F32),
            pltpu.VMEM((2, NCOL, w_rows, 128), F32),
            DMA((2,)),
            DMA((COPIES,)),
            DMA((COPIES,)),
        ],
        compiler_params=pltpu.CompilerParams(
            collective_id=0, has_side_effects=True, vmem_limit_bytes=56 << 20
        ),
        name="layer_backward",
    )(
        tile_coords[0, 0],
        tile_count,
        features,
        weight,
        grad_out,
        tile_values[0, 0],
    )


def solution(mesh):
    return jax.shard_map(
        body,
        mesh=mesh,
        in_specs=(
            P(("col", "row"), None),
            P(),
            P(("col", "row"), None),
            P("col", "row", None, None, None),
            P("col", "row", None, None),
            P("col", "row"),
        ),
        out_specs=(P(("col", "row"), None), P()),
        check_vma=False,
    )
```

time: 849 us -> 109 us (0.13)
  waiting for transfers between devices: 736 us -> 0 us
  Pallas kernels: 0 us -> 104 us
  other arithmetic: 54.5 us -> 0 us
  matrix products: 22.9 us -> 0 us
  local copies, waits for them, and re-layouts: 18.4 us -> 3.14 us
  between operations: 14.5 us -> 1.29 us
    psum x1 -> x0, waiting for transfers between devices: 411 us -> none  [body(): weight_grad = lax.psum(local_weight, ('col', 'row')) * scaling]
    reduce_scatter x2 -> x0, waiting for transfers between devices: 189 us -> none  [the longest x1 105 us: body(): lax.psum_scatter(transposed.astype(jnp.bfloat16), 'row', scatter_dimensio...]
    all_gather x2 -> x0, waiting for transfers between devices: 135 us -> none  [the longest x1 77.5 us: body(): column_rows = lax.all_gather(features, 'row', axis=0, tiled=True)]
    pallas_call x0 -> x1, Pallas kernels: none -> 104 us  [body(): pl.pallas_call(functools.partial(kernel, PIECES, 1.0 / math.sqrt(nodes)),...]
    scatter-add x2 -> x0, other arithmetic: 47.1 us -> none  [the longest x1 28.7 us: backward_tiles(): summed = jax.ops.segment_sum(product, tile_pairs[1], num_segments=col_tiles)]
    dot_general x5 -> x0, matrix products: 22.9 us -> none  [the longest x1 10.1 us: backward_tiles(): jnp.einsum('sab,saf->sbf', masked, picked, preferred_element_type=jnp.flo...]
    gather x2 -> x0, local copies, waits for them, and re-layouts: 15 us -> none  [the longest x1 7.7 us: forward_tiles(): picked = column_rows.reshape(-1, tile_size, feat_width)[tile_pairs[1]]]
  transfers between devices with their start and end apart: 5 -> 0, of which waited for: 5 -> 0; matrix products, arithmetic and copies ran while one was open for 7% -> 0% of each run, Pallas kernels for 0% -> 0%
where the time goes in v1:
time: 109 us
  Pallas kernels  104 us (95%)
  local copies, waits for them, and re-layouts  3.14 us (3%)
  between operations  1.29 us (1%)
    pallas_call x1, Pallas kernels, body(): pl.pallas_call(functools.partial(kernel, PIECES, 1.0 / math.sqrt(nodes)),...  104 us
    unnamed x2, local copies, waits for them, and re-layouts  3.14 us

profile of v1, /device:TPU:1, one launch (start us, length us, event | category | flops | bytes accessed | tf_op | source)
XLA Modules:
  0.0 108.6 jit_solution(3410656619172221872)
XLA Ops:
  1.3 104.2 %layer_backward.1 = (bf16[128,256]{1,0:T(8,128)(2,1)}, f32[256,256]{1,0:T(8,128)}) custom-call(s32[2,96]{1,0:T(2,128)} %bitcast.3, s32[1,1]{1,0:T(1,128)S(6)} %copy.10.count_ref, bf16[128,256]{1,0:T(8,128)(2,1)} %feat_ref.1, bf16[256,256]{1,0:T(8,128)(2,1)} %weight_ref.1, bf16[128,256]{1,0:T(8,128)(2,1)} %grad_ref.1, bf16[96,128,128]{2,1,0:T(8,128)(2,1)} %bitcast.2), custom_call_target="tpu_custom_call" | custom-call | tf_op jit(solution)/shard_map/layer_backward/pallas_call | solution.py:441
  105.5 1.5 %copy.11 = bf16[128,256]{1,0:T(8,128)(2,1)} copy(bf16[128,256]{1,0:T(8,128)(2,1)} %get-tuple-element.4) | data formatting | bytes 131072
  107.0 1.7 %copy.12 = f32[256,256]{1,0:T(8,128)} copy(f32[256,256]{1,0:T(8,128)} %get-tuple-element.5) | data formatting | bytes 524288

commit v2 on v1

v2 whole, which is shorter than its diff:
```python
import functools
import math

import jax
import jax.numpy as jnp
from jax import lax
from jax.experimental import pallas as pl
from jax.experimental.pallas import tpu as pltpu
from jax.sharding import PartitionSpec as P

MESH = pl.DeviceIdType.MESH
DMA = pltpu.SemaphoreType.DMA
BF = jnp.bfloat16
F32 = jnp.float32

SX, SY, SZ = 4, 4, 16
OFFS = (0, 1, -1, 2, -2, 3, -3, 4, -4, 5, -5, 6, -6, 7, -7, 8)
GROUPS = ((0, 1), (1, 5), (5, 9), (9, 13), (13, 16))
SLOT = {o: t for t, o in enumerate(OFFS)}
SLOT[-8] = SLOT[8]
NCOL = SX * SY


class Links:
    def __init__(self, send_sems, recv_sems):
        self.send_sems, self.recv_sems = send_sems, recv_sems
        self.used = 0
        self.sent = []

    def copy(self, src, dst, device):
        at = self.used
        self.used += 1
        return pltpu.make_async_remote_copy(
            src_ref=src,
            dst_ref=dst,
            send_sem=self.send_sems.at[at],
            recv_sem=self.recv_sems.at[at],
            device_id=device,
            device_id_type=MESH,
        )

    def start(self, src, dst, device):
        copy = self.copy(src, dst, device)
        copy.start()
        self.sent.append(copy)
        return copy

    def drain(self):
        for copy in self.sent:
            copy.wait_send()


def kernel(
    pieces,
    scaling,
    coords_ref,
    count_ref,
    feat_ref,
    weight_ref,
    grad_ref,
    tiles_ref,
    out_ref,
    wout_ref,
    inv_v,
    inv_s,
    tiles,
    tiles_t,
    feats,
    acc,
    part,
    part_rx,
    sums,
    sums_rx,
    backs,
    own_t,
    pair_tx,
    pair_rx,
    leaf_tx,
    leaf_rx,
    chain_tx,
    chain_rx,
    w_loc,
    w_rx,
    w_sum,
    w_rx2,
    w_far,
    w_near,
    w_pair,
    w_fin,
    local_sems,
    send_sems,
    recv_sems,
):
    col, row = lax.axis_index("col"), lax.axis_index("row")
    x, y = col // SY, col % SY
    z, core = row // 2, row % 2
    links = Links(send_sems, recv_sems)
    slots = tiles_ref.shape[0]
    tile = tiles_ref.shape[1]
    half = tile // 2

    def at_z(offset):
        return (col, lax.rem(z + offset + SZ, SZ) * 2 + core)

    def col_at(dx, dy):
        return lax.rem(x + dx + SX, SX) * SY + lax.rem(y + dy + SY, SY)

    partner = (col, z * 2 + 1 - core)

    def beside(axis, offset):
        return (col_at(offset, 0) if axis == 0 else col_at(0, offset), row)

    barrier = pltpu.get_barrier_semaphore()
    greeted = [at_z(o) for o in (1, -1, 2, -2, 4, -4, 8)] + [partner]
    greeted += [beside(axis, o) for axis in (0, 1) for o in (1, 2, 3)]
    for device in greeted:
        pl.semaphore_signal(barrier, inc=1, device_id=device, device_id_type=MESH)

    load_tiles = pltpu.make_async_copy(
        tiles_ref, tiles.at[pl.ds(1, slots)], local_sems.at[0]
    )
    load_tiles.start()
    feats[0, 0] = feat_ref[...]
    pl.semaphore_wait(barrier, len(greeted))

    ahead = {}
    rows_of = tile // pieces

    def rows(p):
        return pl.ds(p * rows_of, rows_of)

    def feat_at(t, p):
        return feats.at[t, 0, rows(p)]

    def stride(dist):
        for p in range(pieces):
            for side in (1, -1):
                far = dist + 2
                if dist:
                    ahead[side * dist, p].wait_recv()
                if far == 8 and (p < pieces // 2) != (side == 1):
                    continue
                ahead[side * far, p] = links.start(
                    feat_at(SLOT[side * dist], p),
                    feat_at(SLOT[side * far], p),
                    at_z(side * 2),
                )

    def hand_over(dist):
        for side in (1, -1):
            ahead[side * (dist + 1)] = links.start(
                feats.at[SLOT[side * dist], 0],
                feats.at[SLOT[side * (dist + 1)], 0],
                at_z(side),
            )

    crossed = {}

    def cross(t):
        crossed[t] = links.start(feats.at[t, 0], feats.at[t, 1], partner)

    stride(0)
    hand_over(0)
    cross(0)

    tile_row = lax.broadcasted_iota(jnp.int32, inv_v.shape, 0)
    tile_col = lax.broadcasted_iota(jnp.int32, inv_v.shape, 1)
    live = jnp.broadcast_to(count_ref[...], inv_v.shape)

    def enter(k, table):
        hit = (tile_row == coords_ref[0, k]) & (tile_col == coords_ref[1, k])
        hit = hit & (jnp.full(inv_v.shape, k, jnp.int32) < live)
        return jnp.where(hit, k + 1, table)

    inv_v[...] = lax.fori_loop(
        0, slots, enter, jnp.zeros(inv_v.shape, jnp.int32), unroll=8
    )
    table_copy = pltpu.make_async_copy(inv_v, inv_s, local_sems.at[1])
    table_copy.start()
    tiles[0] = jnp.zeros(tiles.shape[1:], BF)
    tiles_t[0] = jnp.zeros(tiles.shape[1:], BF)
    table_copy.wait()
    load_tiles.wait()

    def column_tile(t, other):
        source = lax.rem(z - OFFS[t] + SZ, SZ)
        return source * 2 + (1 - core if other else core)

    block = 4

    order = [
        (a + i, b + j) for a, b in ((2, 2), (2, 0), (0, 2), (0, 0)) for i in (0, 1) for j in (0, 1)
    ]

    def row_tile_of(q):
        a = 2 - 2 * (q // 8) + q % 4 // 2
        b = 2 - 2 * (q // 4 % 2) + q % 2
        return lax.rem(x + a, SX) * SY + lax.rem(y + b, SY)

    def product(lo, hi, q0):
        columns = [column_tile(t, o) for t in range(lo, hi) for o in (0, 1)]
        lhs = []
        for a in range(block):
            i = row_tile_of(q0 + a)
            lhs.append(jnp.concatenate([tiles[inv_s[i, j]] for j in columns], axis=1))
        rhs = feats[lo:hi].reshape((hi - lo) * 2 * tile, -1)
        return jnp.dot(
            jnp.concatenate(lhs, axis=0), rhs, preferred_element_type=F32
        )

    def accumulate(lo, hi):
        def one(b, carry):
            at = pl.ds(pl.multiple_of(b * block * tile, block * tile), block * tile)
            if lo == 0:
                acc[at] = product(lo, hi, b * block)
            else:
                acc[at] += product(lo, hi, b * block)
            return carry

        lax.fori_loop(0, NCOL // block, one, 0)

    def flip(k, carry):
        tiles_t[k + 1] = tiles[k + 1].T
        return carry

    lax.fori_loop(0, slots, flip, 0, unroll=4)
    for s in range(1, 5):
        if s < 4:
            stride(2 * s)
            hand_over(2 * s)
        else:
            for p in range(pieces):
                ahead[8 if p < pieces // 2 else -8, p].wait_recv()
        for side in (1, -1):
            if s < 4:
                cross(SLOT[side * 2 * s])
            ahead[side * (2 * s - 1)].wait_recv()
            cross(SLOT[side * (2 * s - 1)])
        if s == 4:
            cross(SLOT[8])
        lo, hi = GROUPS[s - 1]
        for t in range(lo, hi):
            crossed[t].wait_recv()
        accumulate(lo, hi)

    lo, hi = GROUPS[-1]
    for t in range(lo, hi):
        crossed[t].wait_recv()

    lanes = [slice(0, 128), slice(128, 256)]
    first = {}
    for b in range(NCOL // block):
        at = pl.ds(b * block * tile, block * tile)
        total = (acc[at] + product(lo, hi, b * block)).astype(BF)
        some = order[b * block : (b + 1) * block]
        for n, (dx, dy) in enumerate(some):
            for axis, (i, w) in enumerate(((dx, dy), (dy, dx))):
                part[axis, i, w] = total[n * tile : (n + 1) * tile, lanes[axis]]
        for axis in (0, 1):
            for i in sorted({d[axis] for d in some}):
                w = min(d[1 - axis] for d in some)
                if i:
                    first[axis, i, w] = links.start(
                        part.at[axis, i, pl.ds(w, 2)],
                        part_rx.at[axis, i, pl.ds(w, 2)],
                        beside(axis, i),
                    )
    second = {}
    own_sum = {}
    for w0 in (2, 0):
        for axis in (0, 1):
            for i in (1, 2, 3):
                first[axis, i, w0].wait_recv()
            for w in (w0 + 1, w0) if w0 == 0 else (w0, w0 + 1):
                mine = part[axis, 0, w].astype(F32)
                for i in (1, 2, 3):
                    mine = mine + part_rx[axis, i, w].astype(F32)
                if w:
                    sums[axis, w] = mine.astype(BF)
                    second[axis, w] = links.start(
                        sums.at[axis, w], sums_rx.at[axis, w], beside(1 - axis, w)
                    )
                else:
                    own_sum[axis] = mine
    halves = []
    for axis in (0, 1):
        mine = own_sum[axis]
        for w in (2, 3, 1):
            second[axis, w].wait_recv()
            mine = mine + sums_rx[axis, w].astype(F32)
        halves.append(mine)
    agg = jnp.concatenate(halves, axis=1)
    agg = agg.astype(BF)

    weight = weight_ref[...]
    pre_act = jnp.dot(agg, weight, preferred_element_type=F32)
    sigmoid_z = jax.nn.sigmoid(pre_act)
    factor = sigmoid_z * (1.0 + pre_act * (1.0 - sigmoid_z))
    dz = (grad_ref[...].astype(F32) * factor).astype(BF)
    back = lax.dot_general(
        dz, weight, (((1,), (1,)), ((), ())), preferred_element_type=F32
    ).astype(BF)
    for axis in (0, 1):
        backs[axis, 0, 0] = back[:, lanes[axis]]

    for i in (2, 1, 3):
        for axis in (0, 1):
            first[axis, i] = links.start(
                backs.at[axis, 0, 0], backs.at[axis, 0, i], beside(axis, i)
            )
    for w in (2, 1, 3):
        for axis in (0, 1):
            second[axis, w, 0] = links.start(
                backs.at[axis, 0, 0], backs.at[axis, w, 0], beside(1 - axis, w)
            )
    local_weight = lax.dot_general(
        agg, dz, (((0,), (0,)), ((), ())), preferred_element_type=F32
    )
    w_loc[...] = local_weight.astype(BF).reshape(w_loc.shape)
    w_first = {}
    for i in (2, 1, 3):
        to = lax.rem(x + i, SX)
        w_first[i] = links.start(w_loc.at[to], w_rx.at[i - 1], beside(0, i))
    for i in (1, 3, 2):
        for axis in (0, 1):
            first[axis, i].wait_recv()
    for w in (2, 1, 3):
        for axis in (0, 1):
            second[axis, w, 1] = links.start(
                backs.at[axis, 0, pl.ds(1, 3)],
                backs.at[axis, w, pl.ds(1, 3)],
                beside(1 - axis, w),
            )

    w_part = w_loc[x].astype(F32)
    for i in (1, 2, 3):
        w_first[i].wait_recv()
        w_part = w_part + w_rx[i - 1].astype(F32)
    w_sum[...] = w_part.astype(BF)
    w_second = {}
    for i in (2, 1, 3):
        to = lax.rem(y + i, SY)
        w_second[i] = links.start(w_sum.at[to], w_rx2.at[i - 1], beside(1, i))

    for axis in (0, 1):
        for w in (1, 3, 2):
            second[axis, w, 0].wait_recv()
            second[axis, w, 1].wait_recv()

    def back_tile_of(d):
        return lax.rem(x - d // SY + SX, SX) * SY + lax.rem(y - d % SY + SY, SY)

    def whole_back():
        left = [backs[0, d % SY, d // SY] for d in range(NCOL)]
        right = [backs[1, d // SY, d % SY] for d in range(NCOL)]
        return jnp.concatenate(
            [jnp.concatenate(left, axis=0), jnp.concatenate(right, axis=0)], axis=1
        )

    def transposed(columns):
        lhs = []
        for j in columns:
            lhs.append(
                jnp.concatenate(
                    [tiles_t[inv_s[back_tile_of(d), j]] for d in range(NCOL)], axis=1
                )
            )
        return jnp.dot(
            jnp.concatenate(lhs, axis=0),
            whole_back(),
            preferred_element_type=F32,
        )

    pair = {}

    def compute(offsets):
        for t0 in range(0, len(offsets), 2):
            some = offsets[t0 : t0 + 2]
            targets = [lax.rem(z + o + SZ, SZ) * 2 for o in some]
            terms = transposed(
                [t + 1 - core for t in targets] + [t + core for t in targets]
            )
            for n, o in enumerate(some):
                t = SLOT[o]
                pair_tx[t] = terms[n * tile : (n + 1) * tile].astype(BF)
                pair[t] = links.start(pair_tx.at[t], pair_rx.at[t], partner)
                m = n + len(some)
                own_t[t] = terms[m * tile : (m + 1) * tile]

    def pair_sum(o):
        t = SLOT[o]
        pair[t].wait_recv()
        return own_t[t] + pair_rx[t].astype(F32)

    leaf, chain = {}, {}

    def send_leaves(dist):
        for n, side in enumerate((1, -1)):
            m = dist // 2
            leaf_tx[n, m] = pair_sum(side * dist).astype(BF)
            leaf[side, dist] = links.start(
                leaf_tx.at[n, m], leaf_rx.at[n, m], at_z(side)
            )

    def send_chain(dist):
        m = dist // 2 - 1
        for n, side in enumerate((1, -1)):
            total = None if dist == 8 and n else pair_sum(side * dist)
            if total is None:
                total = eighth
            elif dist == 8:
                eighth = total
            else:
                leaf[side, dist + 1].wait_recv()
                total = total + leaf_rx[n, m + 1].astype(F32)
            for h in (n, 1 - n):
                at = pl.ds(h * half, half)
                mine = total[h * half : (h + 1) * half]
                if dist == 8 and h != n:
                    continue
                if dist < 6 or dist == 6 and h == n:
                    chain[side, dist + 2, h].wait_recv()
                    mine = mine + chain_rx[n, m + 1, at].astype(F32)
                chain_tx[n, m, at] = mine.astype(BF)
                chain[side, dist, h] = links.start(
                    chain_tx.at[n, m, at], chain_rx.at[n, m, at], at_z(2 * side)
                )

    compute([8, 7, -7])
    w_own = w_sum[y].astype(F32)
    for i in (1, 2, 3):
        w_second[i].wait_recv()
        w_own = w_own + w_rx2[i - 1].astype(F32)
    group, place = z // 4, z % 4
    w_far[group] = w_own.astype(BF)
    for i in (8, 4, -4):
        w_first[i] = links.start(w_far.at[group], w_far.at[group], at_z(i))
    compute([6, -6, 5, -5])
    send_chain(8)
    send_leaves(7)
    compute([4, -4, 3, -3])
    send_leaves(5)
    compute([2, -2, 1, -1])
    send_leaves(3)
    compute([0])
    send_chain(6)
    for i in (8, 4, -4):
        w_first[i].wait_recv()
    w_near[place] = jnp.sum(w_far[...].astype(F32), axis=0).astype(BF)
    for i in (2, 1, -1):
        w_second[i] = links.start(w_near.at[place], w_near.at[place], at_z(i))
    send_leaves(1)
    send_chain(4)
    for i in (2, 1, -1):
        w_second[i].wait_recv()
    w_pair[0] = jnp.sum(w_near[...].astype(F32), axis=0)
    w_cross = links.start(w_pair.at[0], w_pair.at[1], partner)
    w_cross.wait_recv()
    w_fin[x, y] = (w_pair[0] + w_pair[1]) * scaling
    for i in (2, 1, 3):
        w_first[i] = links.start(w_fin.at[x, y], w_fin.at[x, y], beside(1, i))
    send_chain(2)
    for i in (1, 3, 2):
        w_first[i].wait_recv()
    for i in (2, 1, 3):
        w_second[i] = links.start(w_fin.at[x], w_fin.at[x], beside(0, i))
    total = pair_sum(0)
    for n, side in enumerate((1, -1)):
        leaf[side, 1].wait_recv()
        total = total + leaf_rx[n, 0].astype(F32)
    for n, side in enumerate((1, -1)):
        for h in (n, 1 - n):
            chain[side, 2, h].wait_recv()
        total = total + chain_rx[n, 0].astype(F32)
    out_ref[...] = total.astype(BF)
    for i in (1, 3, 2):
        w_second[i].wait_recv()
    wout_ref[...] = w_fin[...].reshape(wout_ref.shape)
    links.drain()


PIECES = 2
COPIES = 192


def hand_out(a_ref, b_ref, c_ref, d_ref):
    c_ref[...] = a_ref[...]
    d_ref[...] = b_ref[...]


def body(features, weight, grad_out, tile_values, tile_coords, tile_count):
    tile, width = features.shape
    slots = tile_values.shape[2]
    nodes = tile * lax.axis_size("col") * lax.axis_size("row")
    vmem = pl.BlockSpec(memory_space=pltpu.VMEM)
    smem = pl.BlockSpec(memory_space=pltpu.SMEM)
    square = (tile, tile)
    slab = (tile, width)
    w_piece = (width // NCOL, width)
    done = pl.pallas_call(
        functools.partial(kernel, PIECES, 1.0 / math.sqrt(nodes)),
        out_shape=(
            jax.ShapeDtypeStruct(slab, BF),
            jax.ShapeDtypeStruct((width, width), F32),
        ),
        in_specs=[smem, vmem, vmem, vmem, vmem, pl.BlockSpec(memory_space=pl.ANY)],
        out_specs=(vmem, vmem),
        scratch_shapes=[
            pltpu.VMEM((16, 128), jnp.int32),
            pltpu.SMEM((16, 128), jnp.int32),
            pltpu.VMEM((slots + 1,) + square, BF),
            pltpu.VMEM((slots + 1,) + square, BF),
            pltpu.VMEM((16, 2) + slab, BF),
            pltpu.VMEM((NCOL * tile, width), F32),
            pltpu.VMEM((2, 4, 4) + square, BF),
            pltpu.VMEM((2, 4, 4) + square, BF),
            pltpu.VMEM((2, 4) + square, BF),
            pltpu.VMEM((2, 4) + square, BF),
            pltpu.VMEM((2, 4, 4) + square, BF),
            pltpu.VMEM((16,) + slab, F32),
            pltpu.VMEM((16,) + slab, BF),
            pltpu.VMEM((16,) + slab, BF),
            pltpu.VMEM((2, 4) + slab, BF),
            pltpu.VMEM((2, 4) + slab, BF),
            pltpu.VMEM((2, 4) + slab, BF),
            pltpu.VMEM((2, 4) + slab, BF),
            pltpu.VMEM((4, 4) + w_piece, BF),
            pltpu.VMEM((3, 4) + w_piece, BF),
            pltpu.VMEM((4,) + w_piece, BF),
            pltpu.VMEM((3,) + w_piece, BF),
            pltpu.VMEM((4,) + w_piece, BF),
            pltpu.VMEM((4,) + w_piece, BF),
            pltpu.VMEM((2,) + w_piece, F32),
            pltpu.VMEM((4, 4) + w_piece, F32),
            DMA((2,)),
            DMA((COPIES,)),
            DMA((COPIES,)),
        ],
        compiler_params=pltpu.CompilerParams(
            collective_id=0, has_side_effects=True, vmem_limit_bytes=56 << 20
        ),
        name="layer_backward",
    )(
        tile_coords[0, 0],
        tile_count,
        features,
        weight,
        grad_out,
        tile_values[0, 0],
    )
    return pl.pallas_call(
        hand_out,
        out_shape=tuple(jax.ShapeDtypeStruct(a.shape, a.dtype) for a in done),
        in_specs=[vmem, vmem],
        out_specs=(vmem, vmem),
        name="hand_out",
    )(*done)


def solution(mesh):
    return jax.shard_map(
        body,
        mesh=mesh,
        in_specs=(
            P(("col", "row"), None),
            P(),
            P(("col", "row"), None),
            P("col", "row", None, None, None),
            P("col", "row", None, None),
            P("col", "row"),
        ),
        out_specs=(P(("col", "row"), None), P()),
        check_vma=False,
    )
```

time: 109 us -> 94.4 us (0.87)
  Pallas kernels: 104 us -> 93 us
  local copies, waits for them, and re-layouts: 3.14 us -> 0 us
    pallas_call x1, Pallas kernels: 104 us -> 91.2 us  [body(): pl.pallas_call(functools.partial(kernel, PIECES, 1.0 / math.sqrt(nodes)),...]
    unnamed x2 -> x0, local copies, waits for them, and re-layouts: 3.14 us -> none
    pallas_call x0 -> x1, Pallas kernels: none -> 1.72 us  [body(): pl.pallas_call(hand_out, out_shape=tuple((jax.ShapeDtypeStruct(a.shape, a...]
where the time goes in v2:
time: 94.4 us; the launch traced here: 94.3 us
  Pallas kernels  93 us (99%)
  between operations  1.29 us (1%)
    pallas_call x1, Pallas kernels, body(): pl.pallas_call(functools.partial(kernel, PIECES, 1.0 / math.sqrt(nodes)),...  91.2 us

profile of v2, /device:TPU:1, one launch (start us, length us, event | category | flops | bytes accessed | tf_op | source)
XLA Modules:
  0.0 94.3 jit_solution(3486158526952711228)
XLA Ops:
  1.3 91.2 %layer_backward.1 = (bf16[128,256]{1,0:T(8,128)(2,1)}, f32[256,256]{1,0:T(8,128)}) custom-call(s32[2,96]{1,0:T(2,128)} %bitcast.3, s32[1,1]{1,0:T(1,128)S(6)} %copy.8.count_ref, bf16[128,256]{1,0:T(8,128)(2,1)} %feat_ref.1, bf16[256,256]{1,0:T(8,128)(2,1)} %weight_ref.1, bf16[128,256]{1,0:T(8,128)(2,1)} %grad_ref.1, bf16[96,128,128]{2,1,0:T(8,128)(2,1)} %bitcast.2), custom_call_target="tpu_custom_call" | custom-call | tf_op jit(solution)/shard_map/layer_backward/pallas_call | solution.py:500
  92.5 1.7 %hand_out.1 = (bf16[128,256]{1,0:T(8,128)(2,1)}, f32[256,256]{1,0:T(8,128)}) custom-call(bf16[128,256]{1,0:T(8,128)(2,1)} %get-tuple-element.4.a_ref, f32[256,256]{1,0:T(8,128)} %get-tuple-element.5.b_ref), custom_call_target="tpu_custom_call" | custom-call | tf_op jit(solution)/shard_map/hand_out/pallas_call | solution.py:551

commit v3 on v2

--- a/solution.py
+++ b/solution.py
@@ -61,6 +61,10 @@
     tiles_ref,
     out_ref,
     wout_ref,
+    coords_s,
+    count_s,
+    weight_v,
+    grad_v,
     inv_v,
     inv_s,
     tiles,
@@ -81,11 +85,8 @@
     chain_rx,
     w_loc,
     w_rx,
-    w_sum,
-    w_rx2,
     w_far,
     w_near,
-    w_pair,
     w_fin,
     local_sems,
     send_sems,
@@ -102,6 +103,9 @@
     def at_z(offset):
         return (col, lax.rem(z + offset + SZ, SZ) * 2 + core)
 
+    def across_z(offset):
+        return (col, lax.rem(z + offset + SZ, SZ) * 2 + 1 - core)
+
     def col_at(dx, dy):
         return lax.rem(x + dx + SX, SX) * SY + lax.rem(y + dy + SY, SY)
 
@@ -112,15 +116,41 @@
 
     barrier = pltpu.get_barrier_semaphore()
     greeted = [at_z(o) for o in (1, -1, 2, -2, 4, -4, 8)] + [partner]
-    greeted += [beside(axis, o) for axis in (0, 1) for o in (1, 2, 3)]
+    others = [(d // SY, d % SY) for d in range(NCOL - 1, 0, -1)]
+    greeted += [(col_at(dx, dy), row) for dx, dy in others]
+    greeted += [across_z(o) for o in (1, -1, 2, -2)]
     for device in greeted:
         pl.semaphore_signal(barrier, inc=1, device_id=device, device_id_type=MESH)
 
-    load_tiles = pltpu.make_async_copy(
-        tiles_ref, tiles.at[pl.ds(1, slots)], local_sems.at[0]
+    def load(n, src, dst):
+        copy = pltpu.make_async_copy(src, dst, local_sems.at[n])
+        copy.start()
+        return copy
+
+    load_coords = load(0, coords_ref, coords_s)
+    load_count = load(1, count_ref, count_s)
+    load_feats = load(2, feat_ref, feats.at[0, 0])
+    load_tiles = load(3, tiles_ref, tiles.at[pl.ds(1, slots)])
+    load_weight = load(4, weight_ref, weight_v)
+    load_grad = load(5, grad_ref, grad_v)
+
+    tile_row = lax.broadcasted_iota(jnp.int32, inv_v.shape, 0)
+    tile_col = lax.broadcasted_iota(jnp.int32, inv_v.shape, 1)
+    load_coords.wait()
+    load_count.wait()
+    live = count_s[0, 0]
+
+    def enter(k, table):
+        hit = (tile_row == coords_s[0, k]) & (tile_col == coords_s[1, k])
+        hit = hit & (jnp.full(inv_v.shape, k, jnp.int32) < live)
+        return jnp.where(hit, k + 1, table)
+
+    inv_v[...] = lax.fori_loop(
+        0, slots, enter, jnp.zeros(inv_v.shape, jnp.int32), unroll=8
     )
-    load_tiles.start()
-    feats[0, 0] = feat_ref[...]
+    table_copy = pltpu.make_async_copy(inv_v, inv_s, local_sems.at[6])
+    table_copy.start()
+    load_feats.wait()
     pl.semaphore_wait(barrier, len(greeted))
 
     ahead = {}
@@ -163,20 +193,6 @@
     hand_over(0)
     cross(0)
 
-    tile_row = lax.broadcasted_iota(jnp.int32, inv_v.shape, 0)
-    tile_col = lax.broadcasted_iota(jnp.int32, inv_v.shape, 1)
-    live = jnp.broadcast_to(count_ref[...], inv_v.shape)
-
-    def enter(k, table):
-        hit = (tile_row == coords_ref[0, k]) & (tile_col == coords_ref[1, k])
-        hit = hit & (jnp.full(inv_v.shape, k, jnp.int32) < live)
-        return jnp.where(hit, k + 1, table)
-
-    inv_v[...] = lax.fori_loop(
-        0, slots, enter, jnp.zeros(inv_v.shape, jnp.int32), unroll=8
-    )
-    table_copy = pltpu.make_async_copy(inv_v, inv_s, local_sems.at[1])
-    table_copy.start()
     tiles[0] = jnp.zeros(tiles.shape[1:], BF)
     tiles_t[0] = jnp.zeros(tiles.shape[1:], BF)
     table_copy.wait()
@@ -292,11 +308,13 @@
     agg = jnp.concatenate(halves, axis=1)
     agg = agg.astype(BF)
 
-    weight = weight_ref[...]
+    load_weight.wait()
+    load_grad.wait()
+    weight = weight_v[...]
     pre_act = jnp.dot(agg, weight, preferred_element_type=F32)
     sigmoid_z = jax.nn.sigmoid(pre_act)
     factor = sigmoid_z * (1.0 + pre_act * (1.0 - sigmoid_z))
-    dz = (grad_ref[...].astype(F32) * factor).astype(BF)
+    dz = (grad_v[...].astype(F32) * factor).astype(BF)
     back = lax.dot_general(
         dz, weight, (((1,), (1,)), ((), ())), preferred_element_type=F32
     ).astype(BF)
@@ -317,10 +335,12 @@
         agg, dz, (((0,), (0,)), ((), ())), preferred_element_type=F32
     )
     w_loc[...] = local_weight.astype(BF).reshape(w_loc.shape)
-    w_first = {}
-    for i in (2, 1, 3):
-        to = lax.rem(x + i, SX)
-        w_first[i] = links.start(w_loc.at[to], w_rx.at[i - 1], beside(0, i))
+    w_copies = {}
+    for n, (dx, dy) in enumerate(others):
+        to = (lax.rem(x + dx, SX), lax.rem(y + dy, SY))
+        w_copies[n] = links.start(
+            w_loc.at[to[0], to[1]], w_rx.at[n], (col_at(dx, dy), row)
+        )
     for i in (1, 3, 2):
         for axis in (0, 1):
             first[axis, i].wait_recv()
@@ -332,15 +352,14 @@
                 beside(1 - axis, w),
             )
 
-    w_part = w_loc[x].astype(F32)
-    for i in (1, 2, 3):
-        w_first[i].wait_recv()
-        w_part = w_part + w_rx[i - 1].astype(F32)
-    w_sum[...] = w_part.astype(BF)
-    w_second = {}
-    for i in (2, 1, 3):
-        to = lax.rem(y + i, SY)
-        w_second[i] = links.start(w_sum.at[to], w_rx2.at[i - 1], beside(1, i))
+    w_own = w_loc[x, y].astype(F32)
+    for n in range(len(others)):
+        w_copies[n].wait_recv()
+        w_own = w_own + w_rx[n].astype(F32)
+    group, place = z // 4, z % 4
+    w_far[group] = w_own.astype(BF)
+    for i in (8, 4, -4):
+        w_copies[i] = links.start(w_far.at[group], w_far.at[group], at_z(i))
 
     for axis in (0, 1):
         for w in (1, 3, 2):
@@ -404,21 +423,20 @@
 
     def send_chain(dist):
         m = dist // 2 - 1
+        totals = []
         for n, side in enumerate((1, -1)):
-            total = None if dist == 8 and n else pair_sum(side * dist)
-            if total is None:
-                total = eighth
-            elif dist == 8:
-                eighth = total
+            if dist == 8:
+                totals.append(totals[0] if n else pair_sum(8))
             else:
+                total = pair_sum(side * dist)
                 leaf[side, dist + 1].wait_recv()
-                total = total + leaf_rx[n, m + 1].astype(F32)
-            for h in (n, 1 - n):
+                totals.append(total + leaf_rx[n, m + 1].astype(F32))
+        for turn in range(1 if dist == 8 else 2):
+            for n, side in enumerate((1, -1)):
+                h = (n + turn) % 2
                 at = pl.ds(h * half, half)
-                mine = total[h * half : (h + 1) * half]
-                if dist == 8 and h != n:
-                    continue
-                if dist < 6 or dist == 6 and h == n:
+                mine = totals[n][h * half : (h + 1) * half]
+                if dist < 6 or dist == 6 and turn == 0:
                     chain[side, dist + 2, h].wait_recv()
                     mine = mine + chain_rx[n, m + 1, at].astype(F32)
                 chain_tx[n, m, at] = mine.astype(BF)
@@ -426,44 +444,38 @@
                     chain_tx.at[n, m, at], chain_rx.at[n, m, at], at_z(2 * side)
                 )
 
-    compute([8, 7, -7])
-    w_own = w_sum[y].astype(F32)
-    for i in (1, 2, 3):
-        w_second[i].wait_recv()
-        w_own = w_own + w_rx2[i - 1].astype(F32)
-    group, place = z // 4, z % 4
-    w_far[group] = w_own.astype(BF)
+    compute([8])
+    compute([7, -7])
+    send_chain(8)
+    compute([6, -6])
+    send_leaves(7)
+    compute([5, -5])
+    compute([4, -4])
+    send_leaves(5)
+    compute([3, -3])
+    send_chain(6)
+    send_leaves(3)
     for i in (8, 4, -4):
-        w_first[i] = links.start(w_far.at[group], w_far.at[group], at_z(i))
-    compute([6, -6, 5, -5])
-    send_chain(8)
-    send_leaves(7)
-    compute([4, -4, 3, -3])
-    send_leaves(5)
-    compute([2, -2, 1, -1])
-    send_leaves(3)
+        w_copies[i].wait_recv()
+    mine = place * 2 + core
+    w_near[mine] = jnp.sum(w_far[...].astype(F32), axis=0).astype(BF)
+    for n, device in enumerate(
+        [f(o) for o in (2, 1, -1) for f in (at_z, across_z)] + [partner]
+    ):
+        w_copies[n] = links.start(w_near.at[mine], w_near.at[mine], device)
+    compute([2, -2])
+    compute([1, -1])
     compute([0])
-    send_chain(6)
-    for i in (8, 4, -4):
-        w_first[i].wait_recv()
-    w_near[place] = jnp.sum(w_far[...].astype(F32), axis=0).astype(BF)
-    for i in (2, 1, -1):
-        w_second[i] = links.start(w_near.at[place], w_near.at[place], at_z(i))
     send_leaves(1)
     send_chain(4)
-    for i in (2, 1, -1):
-        w_second[i].wait_recv()
-    w_pair[0] = jnp.sum(w_near[...].astype(F32), axis=0)
-    w_cross = links.start(w_pair.at[0], w_pair.at[1], partner)
-    w_cross.wait_recv()
-    w_fin[x, y] = (w_pair[0] + w_pair[1]) * scaling
-    for i in (2, 1, 3):
-        w_first[i] = links.start(w_fin.at[x, y], w_fin.at[x, y], beside(1, i))
+    for n in range(7):
+        w_copies[n].wait_recv()
+    w_fin[x, y] = (jnp.sum(w_near[...].astype(F32), axis=0) * scaling).astype(BF)
+    for n, (dx, dy) in enumerate(others):
+        w_copies[n] = links.start(
+            w_fin.at[x, y], w_fin.at[x, y], (col_at(dx, dy), row)
+        )
     send_chain(2)
-    for i in (1, 3, 2):
-        w_first[i].wait_recv()
-    for i in (2, 1, 3):
-        w_second[i] = links.start(w_fin.at[x], w_fin.at[x], beside(0, i))
     total = pair_sum(0)
     for n, side in enumerate((1, -1)):
         leaf[side, 1].wait_recv()
@@ -473,9 +485,9 @@
             chain[side, 2, h].wait_recv()
         total = total + chain_rx[n, 0].astype(F32)
     out_ref[...] = total.astype(BF)
-    for i in (1, 3, 2):
-        w_second[i].wait_recv()
-    wout_ref[...] = w_fin[...].reshape(wout_ref.shape)
+    for n in range(len(others)):
+        w_copies[n].wait_recv()
+    wout_ref[...] = w_fin[...].astype(F32).reshape(wout_ref.shape)
     links.drain()
 
 
@@ -493,7 +505,6 @@
     slots = tile_values.shape[2]
     nodes = tile * lax.axis_size("col") * lax.axis_size("row")
     vmem = pl.BlockSpec(memory_space=pltpu.VMEM)
-    smem = pl.BlockSpec(memory_space=pltpu.SMEM)
     square = (tile, tile)
     slab = (tile, width)
     w_piece = (width // NCOL, width)
@@ -503,9 +514,13 @@
             jax.ShapeDtypeStruct(slab, BF),
             jax.ShapeDtypeStruct((width, width), F32),
         ),
-        in_specs=[smem, vmem, vmem, vmem, vmem, pl.BlockSpec(memory_space=pl.ANY)],
+        in_specs=[pl.BlockSpec(memory_space=pltpu.HBM)] * 6,
         out_specs=(vmem, vmem),
         scratch_shapes=[
+            pltpu.SMEM((2, slots), jnp.int32),
+            pltpu.SMEM((1, 1), jnp.int32),
+            pltpu.VMEM((width, width), BF),
+            pltpu.VMEM(slab, BF),
             pltpu.VMEM((16, 128), jnp.int32),
             pltpu.SMEM((16, 128), jnp.int32),
             pltpu.VMEM((slots + 1,) + square, BF),
@@ -525,14 +540,11 @@
             pltpu.VMEM((2, 4) + slab, BF),
             pltpu.VMEM((2, 4) + slab, BF),
             pltpu.VMEM((4, 4) + w_piece, BF),
-            pltpu.VMEM((3, 4) + w_piece, BF),
+            pltpu.VMEM((NCOL - 1,) + w_piece, BF),
             pltpu.VMEM((4,) + w_piece, BF),
-            pltpu.VMEM((3,) + w_piece, BF),
-            pltpu.VMEM((4,) + w_piece, BF),
-            pltpu.VMEM((4,) + w_piece, BF),
-            pltpu.VMEM((2,) + w_piece, F32),
-            pltpu.VMEM((4, 4) + w_piece, F32),
-            DMA((2,)),
+            pltpu.VMEM((8,) + w_piece, BF),
+            pltpu.VMEM((4, 4) + w_piece, BF),
+            DMA((7,)),
             DMA((COPIES,)),
             DMA((COPIES,)),
         ],

time: 94.4 us -> 90.7 us (0.961)
  Pallas kernels: 93 us -> 89.2 us
    pallas_call x1, Pallas kernels: 91.2 us -> 87.5 us  [body(): pl.pallas_call(functools.partial(kernel, PIECES, 1.0 / math.sqrt(nodes)),...]
where the time goes in v3:
time: 90.7 us; the launch traced here: 90.5 us
  Pallas kernels  89.2 us (98%)
  between operations  1.29 us (1%)
    pallas_call x1, Pallas kernels, body(): pl.pallas_call(functools.partial(kernel, PIECES, 1.0 / math.sqrt(nodes)),...  87.5 us

profile of v3, /device:TPU:1, one launch (start us, length us, event | category | flops | bytes accessed | tf_op | source)
XLA Modules:
  0.0 90.5 jit_solution(5986329536609128795)
XLA Ops:
  1.3 87.5 %layer_backward.1 = (bf16[128,256]{1,0:T(8,128)(2,1)}, f32[256,256]{1,0:T(8,128)}) custom-call(s32[2,96]{1,0:T(2,128)} %bitcast.3, s32[1,1]{1,0:T(1,128)S(6)} %copy.8.count_ref, bf16[128,256]{1,0:T(8,128)(2,1)} %feat_ref.1, bf16[256,256]{1,0:T(8,128)(2,1)} %weight_ref.1, bf16[128,256]{1,0:T(8,128)(2,1)} %grad_ref.1, bf16[96,128,128]{2,1,0:T(8,128)(2,1)} %bitcast.2), custom_call_target="tpu_custom_call" | custom-call | tf_op jit(solution)/shard_map/layer_backward/pallas_call | solution.py:511
  88.8 1.7 %hand_out.1 = (bf16[128,256]{1,0:T(8,128)(2,1)}, f32[256,256]{1,0:T(8,128)}) custom-call(bf16[128,256]{1,0:T(8,128)(2,1)} %get-tuple-element.4.a_ref, f32[256,256]{1,0:T(8,128)} %get-tuple-element.5.b_ref), custom_call_target="tpu_custom_call" | custom-call | tf_op jit(solution)/shard_map/hand_out/pallas_call | solution.py:563

commit v4 on v3

--- a/solution.py
+++ b/solution.py
@@ -45,13 +45,16 @@
         self.sent.append(copy)
         return copy
 
-    def drain(self):
-        for copy in self.sent:
+    def drain(self, keep=0):
+        cut = len(self.sent) - keep
+        for copy in self.sent[:cut]:
             copy.wait_send()
+        self.sent = self.sent[cut:]
 
 
 def kernel(
     pieces,
+    chain_pieces,
     scaling,
     coords_ref,
     count_ref,
@@ -98,7 +101,7 @@
     links = Links(send_sems, recv_sems)
     slots = tiles_ref.shape[0]
     tile = tiles_ref.shape[1]
-    half = tile // 2
+    chain_rows = tile // chain_pieces
 
     def at_z(offset):
         return (col, lax.rem(z + offset + SZ, SZ) * 2 + core)
@@ -281,6 +284,7 @@
                         part_rx.at[axis, i, pl.ds(w, 2)],
                         beside(axis, i),
                     )
+    links.drain(12)
     second = {}
     own_sum = {}
     for w0 in (2, 0):
@@ -341,6 +345,7 @@
         w_copies[n] = links.start(
             w_loc.at[to[0], to[1]], w_rx.at[n], (col_at(dx, dy), row)
         )
+    links.drain(27)
     for i in (1, 3, 2):
         for axis in (0, 1):
             first[axis, i].wait_recv()
@@ -361,6 +366,7 @@
     for i in (8, 4, -4):
         w_copies[i] = links.start(w_far.at[group], w_far.at[group], at_z(i))
 
+    links.drain(9)
     for axis in (0, 1):
         for w in (1, 3, 2):
             second[axis, w, 0].wait_recv()
@@ -431,12 +437,13 @@
                 total = pair_sum(side * dist)
                 leaf[side, dist + 1].wait_recv()
                 totals.append(total + leaf_rx[n, m + 1].astype(F32))
-        for turn in range(1 if dist == 8 else 2):
+        apart = chain_pieces // 2
+        for turn in range(apart if dist == 8 else chain_pieces):
             for n, side in enumerate((1, -1)):
-                h = (n + turn) % 2
-                at = pl.ds(h * half, half)
-                mine = totals[n][h * half : (h + 1) * half]
-                if dist < 6 or dist == 6 and turn == 0:
+                h = (n * apart + turn) % chain_pieces
+                at = pl.ds(h * chain_rows, chain_rows)
+                mine = totals[n][h * chain_rows : (h + 1) * chain_rows]
+                if dist < 6 or dist == 6 and turn < apart:
                     chain[side, dist + 2, h].wait_recv()
                     mine = mine + chain_rx[n, m + 1, at].astype(F32)
                 chain_tx[n, m, at] = mine.astype(BF)
@@ -467,6 +474,7 @@
     compute([1, -1])
     compute([0])
     send_leaves(1)
+    links.drain(20)
     send_chain(4)
     for n in range(7):
         w_copies[n].wait_recv()
@@ -475,13 +483,15 @@
         w_copies[n] = links.start(
             w_fin.at[x, y], w_fin.at[x, y], (col_at(dx, dy), row)
         )
+    links.drain(15 + 2 * chain_pieces)
     send_chain(2)
+    links.drain(2 * chain_pieces)
     total = pair_sum(0)
     for n, side in enumerate((1, -1)):
         leaf[side, 1].wait_recv()
         total = total + leaf_rx[n, 0].astype(F32)
     for n, side in enumerate((1, -1)):
-        for h in (n, 1 - n):
+        for h in range(chain_pieces):
             chain[side, 2, h].wait_recv()
         total = total + chain_rx[n, 0].astype(F32)
     out_ref[...] = total.astype(BF)
@@ -491,13 +501,9 @@
     links.drain()
 
 
-PIECES = 2
+PIECES = 4
+CHAIN_PIECES = 2
 COPIES = 192
-
-
-def hand_out(a_ref, b_ref, c_ref, d_ref):
-    c_ref[...] = a_ref[...]
-    d_ref[...] = b_ref[...]
 
 
 def body(features, weight, grad_out, tile_values, tile_coords, tile_count):
@@ -508,12 +514,9 @@
     square = (tile, tile)
     slab = (tile, width)
     w_piece = (width // NCOL, width)
-    done = pl.pallas_call(
-        functools.partial(kernel, PIECES, 1.0 / math.sqrt(nodes)),
-        out_shape=(
-            jax.ShapeDtypeStruct(slab, BF),
-            jax.ShapeDtypeStruct((width, width), F32),
-        ),
+    return pl.pallas_call(
+        functools.partial(kernel, PIECES, CHAIN_PIECES, 1.0 / math.sqrt(nodes)),
+        out_shape=(pltpu.VMEM(slab, BF), pltpu.VMEM((width, width), F32)),
         in_specs=[pl.BlockSpec(memory_space=pltpu.HBM)] * 6,
         out_specs=(vmem, vmem),
         scratch_shapes=[
@@ -560,13 +563,6 @@
         grad_out,
         tile_values[0, 0],
     )
-    return pl.pallas_call(
-        hand_out,
-        out_shape=tuple(jax.ShapeDtypeStruct(a.shape, a.dtype) for a in done),
-        in_specs=[vmem, vmem],
-        out_specs=(vmem, vmem),
-        name="hand_out",
-    )(*done)
 
 
 def solution(mesh):

time: 90.7 us -> 87.8 us (0.968)
  Pallas kernels: 89.2 us -> 85.1 us
  local copies, waits for them, and re-layouts: 0 us -> 1.33 us
    pallas_call x2 -> x1, Pallas kernels: 89.2 us -> 85.1 us  [body(): pl.pallas_call(functools.partial(kernel, PIECES, CHAIN_PIECES, 1.0 / math...]
    unnamed x0 -> x2, local copies, waits for them, and re-layouts: none -> 1.33 us
where the time goes in v4:
time: 87.8 us; the launch traced here: 87.7 us
  Pallas kernels  85.1 us (97%)
  local copies, waits for them, and re-layouts  1.33 us (2%)
  between operations  1.29 us (1%)
    pallas_call x1, Pallas kernels, body(): pl.pallas_call(functools.partial(kernel, PIECES, CHAIN_PIECES, 1.0 / math...  85.1 us

profile of v4, /device:TPU:1, one launch (start us, length us, event | category | flops | bytes accessed | tf_op | source)
XLA Modules:
  0.0 87.7 jit_solution(6515943506976842809)
XLA Ops:
  1.3 85.1 %layer_backward.1 = (bf16[128,256]{1,0:T(8,128)(2,1)S(1)}, f32[256,256]{1,0:T(8,128)S(1)}) custom-call(s32[2,96]{1,0:T(2,128)} %bitcast.3, s32[1,1]{1,0:T(1,128)S(6)} %copy.12.count_ref, bf16[128,256]{1,0:T(8,128)(2,1)} %feat_ref.1, bf16[256,256]{1,0:T(8,128)(2,1)} %weight_ref.1, bf16[128,256]{1,0:T(8,128)(2,1)} %grad_ref.1, bf16[96,128,128]{2,1,0:T(8,128)(2,1)} %bitcast.2), custom_call_target="tpu_custom_call" | custom-call | tf_op jit(solution)/shard_map/layer_backward/pallas_call | solution.py:517
  86.4 0.6 copy.10
  87.0 0.7 copy.11

commit v5 on v4

--- a/solution.py
+++ b/solution.py
@@ -346,11 +346,10 @@
             w_loc.at[to[0], to[1]], w_rx.at[n], (col_at(dx, dy), row)
         )
     links.drain(27)
-    for i in (1, 3, 2):
-        for axis in (0, 1):
+    for axis in (0, 1):
+        for i in (1, 3, 2):
             first[axis, i].wait_recv()
-    for w in (2, 1, 3):
-        for axis in (0, 1):
+        for w in (2, 1, 3):
             second[axis, w, 1] = links.start(
                 backs.at[axis, 0, pl.ds(1, 3)],
                 backs.at[axis, w, pl.ds(1, 3)],

time: 87.8 us -> 87.8 us (level)
  no operation moved by 1% of the time
where the time goes in v5:
time: 87.8 us; the launch traced here: 86.9 us
  Pallas kernels  84.3 us (96%)
  local copies, waits for them, and re-layouts  1.33 us (2%)
  between operations  1.29 us (1%)
    pallas_call x1, Pallas kernels, body(): pl.pallas_call(functools.partial(kernel, PIECES, CHAIN_PIECES, 1.0 / math...  84.3 us

profile of v5, /device:TPU:1, one launch (start us, length us, event | category | flops | bytes accessed | tf_op | source)
XLA Modules:
  0.0 86.9 jit_solution(14275554834534553597)
XLA Ops:
  1.3 84.3 %layer_backward.1 = (bf16[128,256]{1,0:T(8,128)(2,1)S(1)}, f32[256,256]{1,0:T(8,128)S(1)}) custom-call(s32[2,96]{1,0:T(2,128)} %bitcast.3, s32[1,1]{1,0:T(1,128)S(6)} %copy.12.count_ref, bf16[128,256]{1,0:T(8,128)(2,1)} %feat_ref.1, bf16[256,256]{1,0:T(8,128)(2,1)} %weight_ref.1, bf16[128,256]{1,0:T(8,128)(2,1)} %grad_ref.1, bf16[96,128,128]{2,1,0:T(8,128)(2,1)} %bitcast.2), custom_call_target="tpu_custom_call" | custom-call | tf_op jit(solution)/shard_map/layer_backward/pallas_call | solution.py:516
  85.6 0.6 copy.10
  86.2 0.7 copy.11
